TPU v7x, 128 devices: a whole 4x4x4 slice. The times are simulated.
128 devices in a mesh: gx: 16 (over y, z), gy: 8 (over x, core).
Axes of the slice: x: 4, y: 4, z: 4, core: 2. Of those that a mesh axis runs over, the one named last changes fastest.
Arguments:
- next_adjoint: float32 [4, 256, 128, 1024], P(None, 'gx', 'gy'), may hold values from -6 to 6
- accumulation: float32 [256, 128, 1024], P('gx', 'gy'), may hold values from 0.5 to 5
- trans_x: float32 [256, 128, 1024], P('gx', 'gy'), may hold values from 0.1 to 2
- trans_y: float32 [256, 128, 1024], P('gx', 'gy'), may hold values from 0.1 to 2
- trans_z: float32 [256, 128, 1024], P('gx', 'gy'), may hold values from 0.1 to 2
- well_owner: int32 [8192, 1], P(('gx', 'gy')), may hold values from 0 to 127; in each aligned block of 64 rows (0 to 63, 64 to 127, ...) no two rows name the same one
- well_site: int32 [8192], P(('gx', 'gy')), may hold values from 0 to 255
- perf_layers: int32 [8192, 16], P(('gx', 'gy')), may hold values from 0 to 1023
- perf_count: int32 [8192], P(('gx', 'gy')), may hold values from 1 to 16
- well_index: float32 [8192, 16], P(('gx', 'gy')), may hold values from 0.5 to 5
- misfit: float32 [8192, 4], P(('gx', 'gy')), may hold values from -6 to 6
Outputs:
- adjoint_field: float32 [4, 256, 128, 1024], P(None, 'gx', 'gy')
- residual: float32 [4, 256, 128, 1024], P(None, 'gx', 'gy')
Inputs may be any that keep to these rules, and one draw needn't show every extreme that they name: `well_owner`: device number d stands at gx index d // (devices along gy) and gy index d % (devices along gy). In each aligned block of 64 rows (the wells of one device) at most 1 row name the same device. The column's offsets in the owner's block are well_site // 16 along the first dimension and well_site % 16 along the second. The first perf_count[w] entries of row w of perf_layers and well_index are the well's perforations; the rest are unused.
All inputs are finite; a program needn't handle non-finite values.
Results may differ from a plain program's by a relative error of at most 0.038.
Values sent between devices are 32-bit elements; how exact they have to be, the bound alone decides.
A program may use at most 320 MiB of HBM per device.

v0:
```python
import jax
import jax.numpy as jnp
from jax import lax
from jax.sharding import PartitionSpec as P

ITERS = 2


def padded_2(cells, sides, width):
    for axis, dim in sides:
        count = lax.axis_size(axis)
        ends = count - 1
        head = lax.slice_in_dim(cells, 0, width, axis=dim)
        tail = lax.slice_in_dim(cells, cells.shape[dim] - width, cells.shape[dim], axis=dim)
        cells = jnp.concatenate(
            [
                lax.ppermute(tail, axis, [(i, (i + 1) % count) for i in range(ends)]),
                cells,
                lax.ppermute(head, axis, [((i + 1) % count, i) for i in range(ends)]),
            ],
            axis=dim,
        )
    return cells


def from_behind(shard, axis, by):
    size = lax.axis_size(axis)
    pairs = [(i, i + by) for i in range(size) if 0 <= i + by < size]
    return lax.ppermute(shard, axis, pairs)


def well_terms(well_index, misfit, perf_count):
    active = (lax.broadcasted_iota(jnp.int32, well_index.shape, 1) < perf_count[:, None]).astype(
        jnp.float32
    )
    return misfit[:, :, None] * (well_index * active)[:, None, :]


def as_field(values):
    return values.reshape(-1, 1, 1, 1)


def operate(field, accumulation, trans_x, trans_y, trans_z, below_x, below_y):
    padded = padded_2(field, (("gx", 1), ("gy", 2)), 1)
    center = padded[:, 1:-1, 1:-1]
    flux_x = trans_x * (padded[:, 2:, 1:-1] - center)
    lower_x = jnp.concatenate(
        [below_x * (center[:, :1] - padded[:, :1, 1:-1]), flux_x[:, :-1]], axis=1
    )
    flux_y = trans_y * (padded[:, 1:-1, 2:] - center)
    lower_y = jnp.concatenate(
        [below_y * (center[:, :, :1] - padded[:, 1:-1, :1]), flux_y[:, :, :-1]], axis=2
    )
    zero_plane = jnp.zeros_like(center[..., :1])
    flux_z = trans_z * (jnp.concatenate([center[..., 1:], zero_plane], axis=3) - center)
    lower_z = jnp.concatenate([zero_plane, flux_z[..., :-1]], axis=3)
    return accumulation * center - flux_x + lower_x - flux_y + lower_y - flux_z + lower_z


def field_dot(first, second):
    return jnp.sum(first * second, axis=(1, 2, 3))


def residual_norms(residual):
    return lax.psum(field_dot(residual, residual), ("gx", "gy"))


def body(
    next_adjoint,
    accumulation,
    trans_x,
    trans_y,
    trans_z,
    well_owner,
    well_site,
    perf_layers,
    perf_count,
    well_index,
    misfit,
):
    components, rows_x, rows_y, layers = next_adjoint.shape
    count_x = lax.axis_size("gx")
    count_y = lax.axis_size("gy")
    devices = count_x * count_y
    well_rows = misfit.shape[0]
    perf_width = well_index.shape[1]
    capacity = (well_rows + devices - 1) // devices
    targets = well_owner[:, 0]
    positions = jnp.arange(well_rows, dtype=jnp.int32)
    earlier = positions[None, :] < positions[:, None]
    matching = targets[:, None] == targets[None, :]
    order_in = jnp.sum((earlier & matching).astype(jnp.int32), axis=1)
    slot_row = targets * capacity + order_in
    contrib = well_terms(well_index, misfit, perf_count).reshape(well_rows, components * perf_width)
    cell_ids = well_site[:, None] * layers + perf_layers
    values_buf = (
        jnp.zeros((devices * capacity, components * perf_width), jnp.float32)
        .at[slot_row]
        .set(contrib)
    )
    cells_buf = jnp.zeros((devices * capacity, perf_width), jnp.int32).at[slot_row].set(cell_ids)
    arrived_values, arrived_cells = (
        lax.all_to_all(values_buf, ("gx", "gy"), split_axis=0, concat_axis=0, tiled=True),
        lax.all_to_all(cells_buf, ("gx", "gy"), split_axis=0, concat_axis=0, tiled=True),
    )
    flat_vals = jnp.transpose(
        arrived_values.reshape(-1, components, perf_width), (1, 0, 2)
    ).reshape(components, -1)
    sources = (
        jnp.zeros((components, rows_x * rows_y * layers), jnp.float32)
        .at[:, arrived_cells.reshape(-1)]
        .add(flat_vals)
    )
    right_side = accumulation[None] * next_adjoint + sources.reshape(
        components, rows_x, rows_y, layers
    )
    plane_x = lax.broadcasted_iota(jnp.int32, trans_x.shape, 0)
    plane_y = lax.broadcasted_iota(jnp.int32, trans_y.shape, 1)
    plane_z = lax.broadcasted_iota(jnp.int32, trans_z.shape, 2)
    tx_eff = jnp.where(
        (lax.axis_index("gx") == count_x - 1) & (plane_x == rows_x - 1), jnp.float32(0.0), trans_x
    )
    ty_eff = jnp.where(
        (lax.axis_index("gy") == count_y - 1) & (plane_y == rows_y - 1), jnp.float32(0.0), trans_y
    )
    tz_eff = jnp.where(plane_z == layers - 1, jnp.float32(0.0), trans_z)
    below_x = from_behind(tx_eff[rows_x - 1 :], "gx", 1)
    below_y = from_behind(ty_eff[:, rows_y - 1 :], "gy", 1)
    solution = jnp.zeros_like(right_side)
    residual = right_side
    direction = right_side
    norm_now = residual_norms(residual)
    for turn_index in range(ITERS):
        image = operate(direction, accumulation, tx_eff, ty_eff, tz_eff, below_x, below_y)
        curved = lax.psum(field_dot(direction, image), ("gx", "gy"))
        step_len = norm_now / curved
        solution = solution + as_field(step_len) * direction
        residual = residual - as_field(step_len) * image
        if turn_index + 1 < ITERS:
            norm_next = residual_norms(residual)
            direction = residual + as_field(norm_next / norm_now) * direction
            norm_now = norm_next
    return (solution, residual)


def solution(mesh):
    placed = (
        P(None, "gx", "gy", None),
        P("gx", "gy", None),
        P("gx", "gy", None),
        P("gx", "gy", None),
        P("gx", "gy", None),
        P(("gx", "gy"), None),
        P(("gx", "gy")),
        P(("gx", "gy"), None),
        P(("gx", "gy")),
        P(("gx", "gy"), None),
        P(("gx", "gy"), None),
    )
    return jax.shard_map(
        body,
        mesh=mesh,
        in_specs=placed,
        out_specs=(P(None, "gx", "gy", None), P(None, "gx", "gy", None)),
        check_vma=False,
    )
```

profile of v0, /device:TPU:1, one launch (start us, length us, event | category | flops | bytes accessed | tf_op | source)
XLA Modules:
  0.0 520.5 jit_solution(16427901959755998490)
XLA Ops:
  5.0 11.5 %all-to-all-start = ((s32[128,1,16]{2,1,0:T(1,128)}), s32[128,1,16]{2,1,0:T(1,128)S(1)}, u32[]{:S(2)}, u32[]{:S(2)}) async-start(s32[128,1,16]{2,1,0:T(1,128)} %bitcast.4), calls=%async_computation | async-start | bytes 131072 | tf_op jit(solution)/shard_map/all_to_all | solution.py:104
  19.3 6.6 %all-to-all-done = s32[128,1,16]{2,1,0:T(1,128)S(1)} async-done(((s32[128,1,16]{2,1,0:T(1,128)}), s32[128,1,16]{2,1,0:T(1,128)S(1)}, u32[]{:S(2)}, u32[]{:S(2)}) %all-to-all-start) | async-done | bytes 8224 | tf_op jit(solution)/shard_map/all_to_all | solution.py:104
  25.9 4.6 all-to-all-start.1
  32.0 4.4 sort
  40.7 79.6 %scatter_custom_fusion.2 = f32[4,262144]{0,1:T(8,128)} fusion(s32[2048]{0:T(1024)S(1)} %get-tuple-element.4, f32[]{:T(128)} %constant.11.clone.1, f32[2048,4]{1,0:T(8,128)S(1)} %copy.79, s32[2048]{0:T(1024)S(1)} %broadcast_clamp_fusion), kind=kCustom, calls=%fused_computation.4 | custom fusion | flops 8192 | bytes 4194308 | tf_op jit(solution)/shard_map/scatter-add | solution.py:112
  120.3 77.8 %copy.80 = f32[4,16,16,1024]{3,2,1,0:T(8,128)} copy(f32[4,16,16,1024]{0,3,2,1:T(8,128)} %bitcast.12) | data formatting | bytes 8388608 | tf_op jit(solution)/shard_map/reshape | solution.py:114
  198.1 4.6 multiply_add_fusion.2
  205.5 4.4 collective-permute-start.2
  228.9 4.4 collective-permute-start.3
  240.0 5.6 %fusion.10 = (f32[4,16,16,1024]{3,2,1,0:T(8,128)}, f32[4,16,16,1024]{3,2,1,0:T(8,128)}, f32[4,16,16,1024]{3,2,1,0:T(8,128)S(1)}) fusion(f32[4,16,16,1024]{3,2,1,0:T(8,128)S(1)} %copy-done.1, f32[4,1,16,1024]{3,2,1,0:T(8,128)S(1)} %collective-permute-done, f32[16,16,1024]{2,1,0:T(8,128)S(1)} %copy.82, f32[4,18,1,1024]{3,2,1,0:T(1,128)S(1)} %copy.86, ...), kind=kLoop, calls=%fused_computation.21 | loop fusion | flops 10485760 | bytes 24932352 | tf_op jit(solution)/shard_map/mul | solution.py:46
  245.6 4.6 slice.113
  250.7 7.7 %multiply_reduce_fusion.2 = (f32[4]{0:T(128)S(1)}, f32[4]{0:T(128)S(1)}, f32[4,16,16,1024]{3,2,1,0:T(8,128)}) fusion(f32[4,16,16,1024]{3,2,1,0:T(8,128)S(1)} %copy-done.1, f32[4,16,16,1023]{3,2,1,0:T(8,128)S(1)} %bitcast.28, f32[4,16,16,1024]{3,2,1,0:T(8,128)S(1)} %get-tuple-element.28, f32[4,16,15,1024]{3,2,1,0:T(8,128)} %bitcast.30, ...), kind=kLoop, calls=%fused_computation.39 | loop fusion | flops 22020088 | bytes 29126688 | tf_op jit(solution)/shard_map/reduce_sum | solution.py:61
  258.4 66.1 %all-reduce.4 = (f32[4]{0:T(128)S(1)}, f32[4]{0:T(128)S(1)}) all-reduce(f32[4]{0:T(128)S(1)} %get-tuple-element.7, f32[4]{0:T(128)S(1)} %get-tuple-element.6), channel_id=1, replica_groups=mesh['gx'=16,'gy'=8] {'gx','gy'}, use_global_device_ids=true, to_apply=%region_5.6 | all-reduce | flops 8 | bytes 64 | tf_op jit(solution)/shard_map/psum | solution.py:65
  324.6 4.5 multiply_reduce_fusion.1
  329.1 62.8 %psum.30 = f32[4]{0:T(128)S(1)} all-reduce(f32[4]{0:T(128)S(1)} %multiply_reduce_fusion.1), channel_id=1, replica_groups=mesh['gx'=16,'gy'=8] {'gx','gy'}, use_global_device_ids=true, to_apply=%region_9.10 | all-reduce | flops 4 | bytes 32 | tf_op jit(solution)/shard_map/psum | solution.py:65
  391.9 4.5 multiply_add_fusion.1
  398.9 4.9 collective-permute-done.7
  405.1 7.8 %collective-permute-done.6 = f32[4,1,16,1024]{3,2,1,0:T(8,128)S(1)} collective-permute-done((f32[4,1,16,1024]{3,2,1,0:T(8,128)S(1)}, f32[4,1,16,1024]{3,2,1,0:T(8,128)S(1)}, u32[]{:S(2)}, u32[]{:S(2)}) %collective-permute-start.6) | collective-permute-done | bytes 262176 | tf_op jit(solution)/shard_map/ppermute | solution.py:19
  413.6 4.1 collective-permute-start.8
  423.0 5.4 %fusion.6 = (f32[4,16,16,1024]{3,2,1,0:T(8,128)}, f32[4,16,16,1024]{3,2,1,0:T(8,128)}, f32[4,16,16,1024]{3,2,1,0:T(8,128)S(1)}) fusion(f32[4,16,16,1024]{3,2,1,0:T(8,128)S(1)} %multiply_add_fusion.1, f32[4,1,16,1024]{3,2,1,0:T(8,128)S(1)} %collective-permute-done.6, f32[16,16,1024]{2,1,0:T(8,128)S(1)} %copy.82, f32[4,18,1,1024]{3,2,1,0:T(1,128)S(1)} %copy.92, ...), kind=kLoop, calls=%fused_computation.13 | loop fusion | flops 10485760 | bytes 24932352 | tf_op jit(solution)/shard_map/mul | solution.py:46
  428.4 4.6 slice.122
  433.5 7.6 %multiply_reduce_fusion = (f32[4]{0:T(128)S(1)}, f32[4,16,16,1024]{3,2,1,0:T(8,128)}) fusion(f32[4,16,16,1024]{3,2,1,0:T(8,128)S(1)} %multiply_add_fusion.1, f32[4,16,16,1023]{3,2,1,0:T(8,128)S(1)} %bitcast.29, f32[4,16,16,1024]{3,2,1,0:T(8,128)S(1)} %get-tuple-element.25, f32[4,16,15,1024]{3,2,1,0:T(8,128)} %bitcast.31, f32[4,16,1,1024]{3,2,1,0:T(1,128)S(1)} %fusion.22, ...), kind=kLoop, calls=%fused_computation.34 | loop fusion | flops 19922940 | bytes 29126672 | tf_op jit(solution)/shard_map/reduce_sum | solution.py:61
  441.1 66.8 %psum.31 = f32[4]{0:T(128)S(1)} all-reduce(f32[4]{0:T(128)S(1)} %get-tuple-element.10), channel_id=1, replica_groups=mesh['gx'=16,'gy'=8] {'gx','gy'}, use_global_device_ids=true, to_apply=%region_11.12 | all-reduce | flops 4 | bytes 32 | tf_op jit(solution)/shard_map/psum | solution.py:135
  508.0 12.4 %multiply_subtract_fusion = (f32[4,16,16,1024]{3,2,1,0:T(8,128)}, f32[4,16,16,1024]{3,2,1,0:T(8,128)}) fusion(f32[4,16,16,1024]{3,2,1,0:T(8,128)} %get-tuple-element.11, f32[4]{0:T(128)S(1)} %div.11, f32[4,16,16,1024]{3,2,1,0:T(8,128)} %copy-done, f32[4,16,16,1024]{3,2,1,0:T(8,128)} %get-tuple-element.12, f32[4]{0:T(128)S(1)} %div.9, ...), kind=kLoop, calls=%fused_computation.32 | loop fusion | flops 7340032 | bytes 25165856 | tf_op jit(solution)/shard_map/sub | solution.py:138
  (87 shorter events, 51.6 us)
Async XLA Ops:
  5.0 20.9 %all-to-all-start = ((s32[128,1,16]{2,1,0:T(1,128)}), s32[128,1,16]{2,1,0:T(1,128)S(1)}, u32[]{:S(2)}, u32[]{:S(2)}) async-start(s32[128,1,16]{2,1,0:T(1,128)} %bitcast.4), calls=%async_computation | async-start | bytes 131072 | tf_op jit(solution)/shard_map/all_to_all | solution.py:104
  25.9 14.0 %all-to-all-start.1 = ((f32[128,1,64]{2,1,0:T(1,128)}), f32[128,1,64]{2,1,0:T(1,128)S(1)}, u32[]{:S(2)}, u32[]{:S(2)}) async-start(f32[128,1,64]{2,1,0:T(1,128)} %bitcast.8), calls=%async_computation.1 | async-start | bytes 131072 | tf_op jit(solution)/shard_map/all_to_all | solution.py:103
  120.3 77.8 %copy-start.3 = (f32[16,16,1024]{2,1,0:T(8,128)S(1)}, f32[16,16,1024]{2,1,0:T(8,128)}, u32[]{:S(2)}) copy-start(f32[16,16,1024]{2,1,0:T(8,128)} %param.12) | copy-start | bytes 3145732
  198.1 11.8 %copy-start.6 = (f32[16,16,1024]{2,1,0:T(8,128)S(1)}, f32[16,16,1024]{2,1,0:T(8,128)}, u32[]{:S(2)}) copy-start(f32[16,16,1024]{2,1,0:T(8,128)} %param.13) | copy-start | bytes 3145732
  202.8 2.0 copy-start
  204.8 13.7 %copy-start.7 = (f32[16,16,1024]{2,1,0:T(8,128)S(1)}, f32[16,16,1024]{2,1,0:T(8,128)}, u32[]{:S(2)}) copy-start(f32[16,16,1024]{2,1,0:T(8,128)} %param.14) | copy-start | bytes 3145732
  205.5 10.7 %collective-permute-start.2 = (f32[4,1,16,1024]{3,2,1,0:T(8,128)}, f32[4,1,16,1024]{3,2,1,0:T(8,128)S(1)}, u32[]{:S(2)}, u32[]{:S(2)}) collective-permute-start(f32[4,1,16,1024]{3,2,1,0:T(8,128)} %slice.112), channel_id=1, source_target_pairs={{0,8},{8,16},{16,24},{24,32},{32,40},{40,48},{48,56},{56,64},{64,7... | collective-permute-start | bytes 786440 | tf_op jit(solution)/shard_map/ppermute | solution.py:17
  210.7 5.5 %collective-permute-start.1 = (f32[1,16,1024]{2,0,1:T(1,128)S(1)}, f32[1,16,1024]{2,0,1:T(1,128)S(1)}, u32[]{:S(2)}, u32[]{:S(2)}) collective-permute-start(f32[1,16,1024]{2,0,1:T(1,128)S(1)} %slice.111), channel_id=1, source_target_pairs={{0,8},{8,16},{16,24},{24,32},{32,40},{40,48},{48,56},{56,64},{64,7... | collective-permute-start | bytes 196616 | tf_op jit(solution)/shard_map/ppermute | solution.py:29
  217.2 8.9 %collective-permute-start = (f32[4,1,16,1024]{3,2,1,0:T(8,128)S(1)}, f32[4,1,16,1024]{3,2,1,0:T(8,128)S(1)}, u32[]{:S(2)}, u32[]{:S(2)}) collective-permute-start(f32[4,1,16,1024]{3,2,1,0:T(8,128)S(1)} %get-tuple-element.27), channel_id=1, source_target_pairs={{8,0},{16,8},{24,16},{32,24},{40,32},{48,40},{56,48},{64,56},{72,6... | collective-permute-start | bytes 786440 | tf_op jit(solution)/shard_map/ppermute | solution.py:19
  219.2 15.4 %copy-start.8 = (f32[16,16,1024]{2,1,0:T(8,128)S(1)}, f32[16,16,1024]{2,1,0:T(8,128)}, u32[]{:S(2)}) copy-start(f32[16,16,1024]{2,1,0:T(8,128)} %param.15) | copy-start | bytes 3145732
  219.2 31.1 %collective-permute-start.4 = (f32[16,1,1024]{2,0,1:T(8,128)S(1)}, f32[16,1,1024]{2,0,1:T(8,128)S(1)}, u32[]{:S(2)}, u32[]{:S(2)}) collective-permute-start(f32[16,1,1024]{2,0,1:T(8,128)S(1)} %slice.114), channel_id=1, source_target_pairs={{0,1},{1,2},{2,3},{3,4},{4,5},{5,6},{6,7},{8,9},{9,10},{10,11},{11... | collective-permute-start | bytes 196616 | tf_op jit(solution)/shard_map/ppermute | solution.py:29
  228.9 10.8 %collective-permute-start.3 = (f32[4,18,1,1024]{3,1,2,0:T(8,128)S(1)}, f32[4,18,1,1024]{3,1,2,0:T(8,128)S(1)}, u32[]{:S(2)}, u32[]{:S(2)}) collective-permute-start(f32[4,18,1,1024]{3,1,2,0:T(8,128)S(1)} %copy.85), channel_id=1, source_target_pairs={{1,0},{2,1},{3,2},{4,3},{5,4},{6,5},{7,6},{9,8},{10,9},{11,10},{12... | collective-permute-start | bytes 884744 | tf_op jit(solution)/shard_map/ppermute | solution.py:19
  233.4 2.6 copy-start.1
  237.2 13.1 %collective-permute-start.5 = (f32[4,18,1,1024]{3,1,2,0:T(8,128)S(1)}, f32[4,18,1,1024]{3,1,2,0:T(8,128)S(1)}, u32[]{:S(2)}, u32[]{:S(2)}) collective-permute-start(f32[4,18,1,1024]{3,1,2,0:T(8,128)S(1)} %copy.87), channel_id=1, source_target_pairs={{0,1},{1,2},{2,3},{3,4},{4,5},{5,6},{6,7},{8,9},{9,10},{10,11},{11... | collective-permute-start | bytes 884744 | tf_op jit(solution)/shard_map/ppermute | solution.py:17
  245.6 5.1 copy-start.4
  396.4 37.1 %copy-start.2 = (f32[4,16,16,1024]{3,2,1,0:T(8,128)}, f32[4,16,16,1024]{3,2,1,0:T(8,128)S(1)}, u32[]{:S(2)}) copy-start(f32[4,16,16,1024]{3,2,1,0:T(8,128)S(1)} %multiply_add_fusion.1) | copy-start | bytes 12582916
  396.5 7.3 %collective-permute-start.7 = (f32[4,1,16,1024]{3,2,1,0:T(8,128)S(1)}, f32[4,1,16,1024]{3,2,1,0:T(8,128)S(1)}, u32[]{:S(2)}, u32[]{:S(2)}) collective-permute-start(f32[4,1,16,1024]{3,2,1,0:T(8,128)S(1)} %slice.121), channel_id=1, source_target_pairs={{0,8},{8,16},{16,24},{24,32},{32,40},{40,48},{48,56},{56,64},{64,7... | collective-permute-start | bytes 786440 | tf_op jit(solution)/shard_map/ppermute | solution.py:17
  403.8 9.1 %collective-permute-start.6 = (f32[4,1,16,1024]{3,2,1,0:T(8,128)S(1)}, f32[4,1,16,1024]{3,2,1,0:T(8,128)S(1)}, u32[]{:S(2)}, u32[]{:S(2)}) collective-permute-start(f32[4,1,16,1024]{3,2,1,0:T(8,128)S(1)} %get-tuple-element.24), channel_id=1, source_target_pairs={{8,0},{16,8},{24,16},{32,24},{40,32},{48,40},{56,48},{64,56},{72,6... | collective-permute-start | bytes 786440 | tf_op jit(solution)/shard_map/ppermute | solution.py:19
  413.6 9.1 %collective-permute-start.8 = (f32[4,18,1,1024]{3,1,2,0:T(8,128)S(1)}, f32[4,18,1,1024]{3,1,2,0:T(8,128)S(1)}, u32[]{:S(2)}, u32[]{:S(2)}) collective-permute-start(f32[4,18,1,1024]{3,1,2,0:T(8,128)S(1)} %copy.91), channel_id=1, source_target_pairs={{1,0},{2,1},{3,2},{4,3},{5,4},{6,5},{7,6},{9,8},{10,9},{11,10},{12... | collective-permute-start | bytes 884744 | tf_op jit(solution)/shard_map/ppermute | solution.py:19
  419.0 14.1 %collective-permute-start.9 = (f32[4,18,1,1024]{3,1,2,0:T(8,128)S(1)}, f32[4,18,1,1024]{3,1,2,0:T(8,128)S(1)}, u32[]{:S(2)}, u32[]{:S(2)}) collective-permute-start(f32[4,18,1,1024]{3,1,2,0:T(8,128)S(1)} %copy.93), channel_id=1, source_target_pairs={{0,1},{1,2},{2,3},{3,4},{4,5},{5,6},{6,7},{8,9},{9,10},{10,11},{11... | collective-permute-start | bytes 884744 | tf_op jit(solution)/shard_map/ppermute | solution.py:17
  428.4 5.1 copy-start.5
where the time goes:
time: 528 us; the launch traced here: 521 us
  blocking collectives  196 us (37%)
  other arithmetic  149 us (28%)
  local copies, waits for them, and re-layouts  99.1 us (19%)
  starting transfers between devices  45.2 us (9%)
  waiting for transfers between devices  30.3 us (6%)
    psum x2, blocking collectives, residual_norms(): return lax.psum(field_dot(residual, residual), ('gx', 'gy'))  129 us
    scatter-add x3, other arithmetic, body(): sources = jnp.zeros((components, rows_x * rows_y * layers), jnp.float32)....  84 us
    reshape x1, local copies, waits for them, and re-layouts, body(): sources.reshape(components, rows_x, rows_y, layers)  77.8 us
    psum x1, blocking collectives, body(): curved = lax.psum(field_dot(direction, image), ('gx', 'gy'))  66.8 us
    reduce_sum x3, other arithmetic, field_dot(): return jnp.sum(first * second, axis=(1, 2, 3))  19.9 us
    sub x1, other arithmetic, body(): residual = residual - as_field(step_len) * image  12.4 us
    ppermute x4, waiting for transfers between devices, padded_2(): lax.ppermute(head, axis, [((i + 1) % count, i) for i in range(ends)])  12.4 us
    all_to_all x1, starting transfers between devices, body(): lax.all_to_all(cells_buf, ('gx', 'gy'), split_axis=0, concat_axis=0, tile...  11.5 us
  transfers between devices with their start and end apart: 12, of which 7 were waited for; matrix products, arithmetic and copies ran while one was open for 7% of the time, Pallas kernels for 0%

commit v1 on v0

v1 whole, which is shorter than its diff:
```python
import jax
import jax.numpy as jnp
from jax import lax
from jax.experimental import pallas as pl
from jax.experimental.pallas import tpu as pltpu
from jax.sharding import PartitionSpec as P

F32 = jnp.float32
BF16 = jnp.bfloat16
MESH = pl.DeviceIdType.MESH
K, CX, CY, NZ = 4, 16, 16, 1024
NGX, NGY = 16, 8
PERF, WELLS = 16, 64
RHS = range(K)


def remote(src, dst, send, recv, axis, index):
    return pltpu.make_async_remote_copy(
        src_ref=src, dst_ref=dst, send_sem=send, recv_sem=recv,
        device_id={axis: index}, device_id_type=MESH,
    )


def lanes():
    return lax.broadcasted_iota(jnp.int32, (8, 128), 1)


def rows():
    return lax.broadcasted_iota(jnp.int32, (8, 128), 0)


def column(ref, lead, y):
    return ref[(*lead, pl.ds(8 * y, 8), slice(None))]


def layer_above(ref, lead, y, here, lane):
    nxt = ref[(*lead, pl.ds(8 * y + 1, 8), slice(None))]
    return pltpu.roll(jnp.where(lane == 0, nxt, here), 127, 1)


def layer_below(ref, lead, y, here, lane):
    prv = ref[(*lead, pl.ds(8 * y - 1, 8), slice(None))]
    return pltpu.roll(jnp.where(lane == 127, prv, here), 1, 1)


def main_kernel(
    na_h, acc_h, tx_h, ty_h, tz_h, own_h, site_h, lay_h, cnt_h, wi_h, mis_h,
    b, q, w, sp,
    na, co, src, diag, txc, tyc, tzc, tzm,
    own, site, lay, cnt, wi, mis, packed, out1, in1, out2, in2, left, right, red_out, red1, red2,
    load_sem, well_sem, s1, r1, s2, r2, hs, hr, as1, ar1, as2, ar2,
):
    gx, gy = lax.axis_index("gx"), lax.axis_index("gy")
    up_x, down_x = lax.rem(gx + 1, NGX), lax.rem(gx + NGX - 1, NGX)
    up_y, down_y = lax.rem(gy + 1, NGY), lax.rem(gy + NGY - 1, NGY)

    wells = [pltpu.make_async_copy(h, v, well_sem.at[i]) for i, (h, v) in enumerate(
        ((own_h, own), (site_h, site), (lay_h, lay), (cnt_h, cnt), (wi_h, wi), (mis_h, mis)))]
    for c in wells:
        c.start()
    coef = [pltpu.make_async_copy(h, co.at[i], load_sem.at[i]) for i, h in enumerate((tx_h, ty_h, tz_h, acc_h))]
    for c in coef:
        c.start()
    fields = [pltpu.make_async_copy(na_h.at[k], na.at[k], load_sem.at[4 + k]) for k in RHS]
    for c in fields:
        c.start()

    barrier = pltpu.get_barrier_semaphore()
    for d in range(1, NGY):
        pl.semaphore_signal(barrier, inc=1, device_id={"gy": lax.rem(gy + d, NGY)}, device_id_type=MESH)
    for d in range(1, NGX):
        pl.semaphore_signal(barrier, inc=1, device_id={"gx": lax.rem(gx + d, NGX)}, device_id_type=MESH)

    for c in wells:
        c.wait()
    used = lax.broadcasted_iota(jnp.int32, (PERF, WELLS), 0) < cnt[...]
    packed[...] = jnp.zeros_like(packed)
    packed[0:16, :] = jnp.where(used, wi[...], 0.0)
    packed[16:32, :] = lay[...].astype(F32)
    packed[32:36, :] = mis[...]
    packed[36:37, :] = site[...].astype(F32)
    owner = own[...]
    place = lax.rem(owner, NGY) * NGX + owner // NGY
    onehot = jnp.where(lax.broadcasted_iota(jnp.int32, (128, WELLS), 0) == place, 1.0, 0.0).astype(F32)
    out1[...] = lax.dot_general(
        onehot, packed[...], (((1,), (1,)), ((), ())),
        precision=lax.Precision.HIGHEST, preferred_element_type=F32,
    ).reshape(NGY, NGX, 128)

    pl.semaphore_wait(barrier, NGX + NGY - 2)

    first = []
    for d in range(1, NGY):
        to = lax.rem(gy + d, NGY)
        first.append(remote(out1.at[to], in1.at[pl.ds(gy * NGX, NGX)], s1.at[d], r1.at[d], "gy", to))
    for c in first:
        c.start()
    in1[pl.ds(gy * NGX, NGX), :] = out1[gy]

    last_x = gx == NGX - 1
    last_y = gy == NGY - 1

    def spread(i, put):
        def at(x, _):
            for t in range(2):
                for c in range(8):
                    put(x, t, c, co[i, x, pl.ds(8 * t, 8), pl.ds(128 * c, 128)])
            return 0
        coef[i].wait()
        lax.fori_loop(0, CX, at, 0)

    def put_x(x, t, c, v):
        txc[x + 1, pl.ds(64 * t + c, 8, stride=8), :] = jnp.where(last_x & (x == CX - 1), 0.0, v)

    def put_y(x, t, c, v):
        if t == 1:
            v = jnp.where(last_y & (rows() == 7), 0.0, v)
        tyc[x, pl.ds(8 + 64 * t + c, 8, stride=8), :] = v

    def put_z(x, t, c, v):
        if c == 7:
            v = jnp.where(lanes() == 127, 0.0, v)
        tzc[x, pl.ds(8 + 64 * t + c, 8, stride=8), :] = v

    def put_a(x, t, c, v):
        diag[x, pl.ds(64 * t + c, 8, stride=8), :] = v

    spread(0, put_x)
    face_tx = remote(txc.at[CX], txc.at[0], hs.at[0], hr.at[0], "gx", up_x)
    face_tx.start()
    spread(1, put_y)
    face_ty = remote(tyc.at[:, pl.ds(8 * CY, 8)], tyc.at[:, pl.ds(0, 8)], hs.at[1], hr.at[1], "gy", up_y)
    face_ty.start()

    for c in first:
        c.wait()
    for to in range(NGX):
        out2[to] = in1[pl.ds(to, NGY, stride=NGX), :]
    second = []
    for d in range(1, NGX):
        to = lax.rem(gx + d, NGX)
        second.append(remote(out2.at[to], in2.at[pl.ds(gx * NGY, NGY)], s2.at[d], r2.at[d], "gx", to))
    for c in second:
        c.start()
    in2[pl.ds(gx * NGY, NGY), :] = out2[gx]

    spread(2, put_z)
    spread(3, put_a)
    face_tx.wait()
    face_ty.wait()
    tzc[:, 0:8, :] = jnp.zeros((CX, 8, 128), F32)

    def diagonal(x, _):
        lane = lanes()
        start = (rows() == 0) & (lane == 0)
        ty_low = column(tyc, (x,), 0)
        for y in range(CY):
            here = column(tzc, (x,), y + 1)
            below = jnp.where(start, 0.0, layer_below(tzc, (x,), y + 1, here, lane))
            tzm[x, pl.ds(8 * y, 8), :] = below
            ty_here = column(tyc, (x,), y + 1)
            diag[x, pl.ds(8 * y, 8), :] = (
                column(diag, (x,), y) + (column(txc, (x + 1,), y) + column(txc, (x,), y))
                + (ty_here + ty_low) + (here + below)
            )
            ty_low = ty_here
        return 0

    lax.fori_loop(0, CX, diagonal, 0)

    for c in second:
        c.wait()

    across = in2[...].T

    def split(v):
        high = v.astype(BF16).astype(F32)
        return high, (v - high)

    mis_high, mis_low = split(across[32:36, :])
    spot = lax.broadcasted_iota(jnp.int32, (256, 128), 0).astype(F32) == across[36:37, :]
    for k in RHS:
        high = jnp.where(spot, mis_high[k : k + 1, :], 0.0).astype(BF16)
        left[pl.ds(256 * k, 256), 0:128] = high
        left[pl.ds(256 * k, 256), 128:256] = high
        left[pl.ds(256 * k, 256), 256:384] = jnp.where(spot, mis_low[k : k + 1, :], 0.0).astype(BF16)

    def terms(t, _):
        lane = lanes().astype(F32)
        at = pl.ds(pl.multiple_of(16 * t, 16), 16)
        high, low = [], []
        for half in range(2):
            tile = in2[pl.ds(pl.multiple_of(16 * t + 8 * half, 8), 8), :]
            total = [jnp.zeros((8, 128), F32) for _ in range(8)]
            for p in range(PERF):
                value = jnp.broadcast_to(tile[:, p : p + 1], (8, 128))
                layer = jnp.broadcast_to(tile[:, 16 + p : 17 + p], (8, 128))
                for c in range(8):
                    total[c] = total[c] + jnp.where(layer == lane + 128.0 * c, value, 0.0)
            total = jnp.concatenate(total, axis=1)
            h, l = split(total)
            high.append(h)
            low.append(l)
        high = jnp.concatenate(high, axis=0).astype(BF16)
        right[at, :] = high
        right[pl.ds(pl.multiple_of(128 + 16 * t, 16), 16), :] = jnp.concatenate(low, axis=0).astype(BF16)
        right[pl.ds(pl.multiple_of(256 + 16 * t, 16), 16), :] = high
        return 0

    lax.fori_loop(0, 8, terms, 0)

    def gather(n, _):
        at = pl.ds(pl.multiple_of(256 * n, 256), 256)
        src[:, at] = jnp.dot(left[...], right[:, at], preferred_element_type=F32)
        return 0

    lax.fori_loop(0, 4, gather, 0)

    for c in fields:
        c.wait()

    def begin(x):
        for k in RHS:
            for t in range(2):
                for c in range(8):
                    at = (pl.ds(8 * t, 8), pl.ds(128 * c, 128))
                    v = co[3, x, *at] * na[k, x, *at] + src[
                        pl.ds(pl.multiple_of(256 * k + 16 * x + 8 * t, 8), 8), pl.ds(128 * c, 128)]
                    b[k, x + 1, pl.ds(8 + 64 * t + c, 8, stride=8), :] = v

    def faces_x(f, at):
        body = pl.ds(8, 128)
        return [
            remote(f.at[:, 1, body], f.at[:, CX + 1, body], hs.at[at], hr.at[at], "gx", down_x),
            remote(f.at[:, CX, body], f.at[:, 0, body], hs.at[at + 1], hr.at[at + 1], "gx", up_x),
        ]

    def faces_y(f, at):
        body = pl.ds(1, CX)
        return [
            remote(f.at[:, body, pl.ds(8, 8)], f.at[:, body, pl.ds(8 * CY + 8, 8)], hs.at[at], hr.at[at], "gy", down_y),
            remote(f.at[:, body, pl.ds(8 * CY, 8)], f.at[:, body, pl.ds(0, 8)], hs.at[at + 1], hr.at[at + 1], "gy", up_y),
        ]

    def loop(lo, hi, fn):
        def body(x, _):
            fn(x)
            return 0
        lax.fori_loop(lo, hi, body, 0)

    def apply(v, put, x, ys, sums):
        lane = lanes()
        sums = list(sums)
        prev = None
        for y in ys:
            cols = (x - 1,)
            d = column(diag, cols, y - 1)
            txp, txl = column(txc, (x,), y - 1), column(txc, (x - 1,), y - 1)
            typ = column(tyc, cols, y)
            tzp, tzl = column(tzc, cols, y), column(tzm, cols, y - 1)
            if prev is None or prev[0] != y - 1:
                prev = (y - 1, column(tyc, cols, y - 1), [column(v, (k, x), y - 1) for k in RHS],
                        [column(v, (k, x), y) for k in RHS])
            _, tyl, low, mid = prev
            high = [column(v, (k, x), y + 1) for k in RHS]
            for k in RHS:
                here = mid[k]
                out = (
                    d * here
                    - (txp * column(v, (k, x + 1), y) + txl * column(v, (k, x - 1), y))
                    - (typ * high[k] + tyl * low[k])
                    - (tzp * layer_above(v, (k, x), y, here, lane) + tzl * layer_below(v, (k, x), y, here, lane))
                )
                put(k, x, y, out)
                sums[k] = sums[k] + here * here
                sums[K + k] = sums[K + k] + here * out
            prev = (y, typ, mid, high)
        return tuple(sums)

    def put_q(k, x, y, out):
        q[k, x, pl.ds(8 * y, 8), :] = out

    def put_w(k, x, y, out):
        w[k, x - 1, pl.ds(8 * (y - 1), 8), :] = out

    def inner(v, put, sums):
        return lax.fori_loop(2, CX, lambda x, s: apply(v, put, x, range(2, CY), s), sums)

    def ends(v, put, sums):
        return lax.fori_loop(0, 2, lambda i, s: apply(v, put, 1 + (CX - 1) * i, range(1, CY + 1), s), sums)

    def sides(v, put, sums):
        return lax.fori_loop(2, CX, lambda x, s: apply(v, put, x, (1, CY), s), sums)

    loop(0, 2, lambda i: begin((CX - 1) * i))
    bx = faces_x(b, 2)
    for c in bx:
        c.start()
    loop(1, CX - 1, begin)
    by = faces_y(b, 4)
    for c in by:
        c.start()

    none = tuple(jnp.zeros((8, 128), F32) for _ in range(2 * K))
    one = inner(b, put_q, none)
    for c in by + bx:
        c.wait()
    one = ends(b, put_q, one)
    qx = faces_x(q, 6)
    for c in qx:
        c.start()
    one = sides(b, put_q, one)
    qy = faces_y(q, 8)
    for c in qy:
        c.start()
    two = inner(q, put_w, none)
    for c in qy:
        c.wait()
    two = sides(q, put_w, two)
    for c in qx:
        c.wait()
    two = ends(q, put_w, two)

    lane1 = lax.broadcasted_iota(jnp.int32, (1, 128), 1)
    line = jnp.zeros((1, 128), F32)
    for i, s in enumerate(one + two):
        line = jnp.where(lane1 == i, jnp.sum(s, keepdims=True), line)
    red_out[0] = line
    red1[gx] = line
    hops = []
    for d in range(1, NGX):
        to = lax.rem(gx + d, NGX)
        hops.append(remote(red_out.at[0], red1.at[gx], as1.at[d], ar1.at[d], "gx", to))
    for c in hops:
        c.start()
    for c in hops:
        c.wait()
    line = jnp.sum(red1[...], axis=0)
    red_out[1] = line
    red2[gy] = line
    hops = []
    for d in range(1, NGY):
        to = lax.rem(gy + d, NGY)
        hops.append(remote(red_out.at[1], red2.at[gy], as2.at[d], ar2.at[d], "gy", to))
    for c in hops:
        c.start()
    for c in hops:
        c.wait()
    line = jnp.sum(red2[...], axis=0)

    rr = line
    bq = pltpu.roll(line, 128 - K, 1)
    qq = pltpu.roll(line, 128 - 2 * K, 1)
    qw = pltpu.roll(line, 128 - 3 * K, 1)
    step0 = rr / bq
    rr1 = step0 * step0 * qq - rr
    grow = 1.0 + rr1 / rr
    step1 = rr1 / (grow * grow * bq - 2.0 * grow * step0 * qq + step0 * step0 * qw)
    sp[0] = step0 + step1 * grow
    sp[1] = step0 * step1


def last_kernel(b, q, w, sp, x_h, r_h, xo, ro, sem):
    ones = [jnp.broadcast_to(sp[0][:, k : k + 1], (8, 128)) for k in RHS]
    twos = [jnp.broadcast_to(sp[1][:, k : k + 1], (8, 128)) for k in RHS]
    copies = []
    step = 4

    def at(x, _):
        for k in RHS:
            for t in range(2):
                for c in range(8):
                    bv = b[k, x + 1, pl.ds(8 + 64 * t + c, 8, stride=8), :]
                    qv = q[k, x + 1, pl.ds(8 + 64 * t + c, 8, stride=8), :]
                    wv = w[k, x, pl.ds(64 * t + c, 8, stride=8), :]
                    to = (k, x, pl.ds(8 * t, 8), pl.ds(128 * c, 128))
                    xo[to] = ones[k] * bv - twos[k] * qv
                    ro[to] = bv - ones[k] * qv + twos[k] * wv
        return 0

    for i in range(CX // step):
        lax.fori_loop(i * step, (i + 1) * step, at, 0)
        part = pl.ds(i * step, step)
        for j, (s, h) in enumerate(((xo, x_h), (ro, r_h))):
            c = pltpu.make_async_copy(s.at[:, part], h.at[:, part], sem.at[2 * i + j])
            c.start()
            copies.append(c)
    for c in copies:
        c.wait()


def body(next_adjoint, accumulation, trans_x, trans_y, trans_z,
         well_owner, well_site, perf_layers, perf_count, well_index, misfit):
    dma = pltpu.SemaphoreType.DMA
    vm = pltpu.VMEM
    field = (K, CX + 2, 8 * (CY + 2), 128)
    plane = (CX, 8 * CY, 128)
    anywhere = pl.BlockSpec(memory_space=pl.ANY)
    inside = pl.BlockSpec(memory_space=pltpu.VMEM)
    b, q, w, sp = pl.pallas_call(
        main_kernel,
        out_shape=(
            pltpu.VMEM(field, F32), pltpu.VMEM(field, F32), pltpu.VMEM((K, *plane), F32), pltpu.VMEM((2, 1, 128), F32),
        ),
        in_specs=[anywhere] * 11,
        out_specs=(inside,) * 4,
        scratch_shapes=[
            vm((K, CX, CY, NZ), F32), vm((4, CX, CY, NZ), F32), vm((K * CX * CY, NZ), F32),
            vm(plane, F32), vm((CX + 1, 8 * CY, 128), F32), vm((CX, 8 * CY + 8, 128), F32),
            vm((CX, 8 * CY + 8, 128), F32), vm(plane, F32),
            vm((1, WELLS), jnp.int32), vm((1, WELLS), jnp.int32), vm((PERF, WELLS), jnp.int32),
            vm((1, WELLS), jnp.int32), vm((PERF, WELLS), F32), vm((K, WELLS), F32),
            vm((128, WELLS), F32), vm((NGY, NGX, 128), F32), vm((NGY * NGX, 128), F32),
            vm((NGX, NGY, 128), F32), vm((NGX * NGY, 128), F32),
            vm((K * CX * CY, 384), BF16), vm((384, NZ), BF16),
            vm((2, 1, 128), F32), vm((NGX, 1, 128), F32), vm((NGY, 1, 128), F32),
            dma((8,)), dma((6,)), dma((NGY,)), dma((NGY,)), dma((NGX,)), dma((NGX,)),
            dma((10,)), dma((10,)), dma((NGX,)), dma((NGX,)), dma((NGY,)), dma((NGY,)),
        ],
        compiler_params=pltpu.CompilerParams(
            collective_id=0, has_side_effects=True, vmem_limit_bytes=40 * 2**20),
        cost_estimate=pl.CostEstimate(flops=60_000_000, bytes_accessed=9_000_000, transcendentals=0),
        name="adjoint_krylov",
    )(next_adjoint, accumulation, trans_x, trans_y, trans_z, well_owner.T, well_site.reshape(1, WELLS),
      perf_layers.T, perf_count.reshape(1, WELLS), well_index.T, misfit.T)
    out = jax.ShapeDtypeStruct((K, CX, CY, NZ), F32)
    return pl.pallas_call(
        last_kernel,
        out_shape=(out, out),
        in_specs=[inside] * 4,
        out_specs=(anywhere, anywhere),
        scratch_shapes=[vm((K, CX, CY, NZ), F32), vm((K, CX, CY, NZ), F32), dma((8,))],
        compiler_params=pltpu.CompilerParams(vmem_limit_bytes=24 * 2**20),
        name="adjoint_result",
    )(b, q, w, sp)


def solution(mesh):
    flat = P(("gx", "gy"))
    rows_of = P(("gx", "gy"), None)
    cells = P("gx", "gy", None)
    many = P(None, "gx", "gy", None)
    return jax.shard_map(
        body,
        mesh=mesh,
        in_specs=(many, cells, cells, cells, cells, rows_of, flat, rows_of, flat, rows_of, rows_of),
        out_specs=(many, many),
        check_vma=False,
    )
```

time: 528 us -> 51.9 us (0.10); the launches traced: 521 us -> 51.8 us
  blocking collectives: 196 us -> 0 us
  other arithmetic: 149 us -> 0 us
  local copies, waits for them, and re-layouts: 99.1 us -> 0 us
  Pallas kernels: 0 us -> 51.2 us
  starting transfers between devices: 45.2 us -> 0 us
  waiting for transfers between devices: 30.3 us -> 0 us
    psum x3 -> x0, blocking collectives: 196 us -> none  [the longest x2 129 us: residual_norms(): return lax.psum(field_dot(residual, residual), ('gx', 'gy'))]
    scatter-add x3 -> x0, other arithmetic: 84 us -> none  [body(): sources = jnp.zeros((components, rows_x * rows_y * layers), jnp.float32)....]
    reshape x4 -> x0, local copies, waits for them, and re-layouts: 78.4 us -> none  [the longest x1 77.8 us: body(): sources.reshape(components, rows_x, rows_y, layers)]
    pallas_call x0 -> x2, Pallas kernels: none -> 51.2 us  [the longest x1 47.2 us: body(): pl.pallas_call(main_kernel, out_shape=(pltpu.VMEM(field, F32), pltpu.VMEM...]
    ppermute x10 -> x0, starting transfers between devices: 29.1 us -> none  [the longest x4 11.2 us: padded_2(): lax.ppermute(tail, axis, [(i, (i + 1) % count) for i in range(ends)])]
    reduce_sum x4 -> x0, other arithmetic: 20.8 us -> none  [the longest x3 19.9 us: field_dot(): return jnp.sum(first * second, axis=(1, 2, 3))]
    ppermute x10 -> x0, waiting for transfers between devices: 20.1 us -> none  [the longest x4 12.4 us: padded_2(): lax.ppermute(head, axis, [((i + 1) % count, i) for i in range(ends)])]
    all_to_all x2 -> x0, starting transfers between devices: 16.1 us -> none  [the longest x1 11.5 us: body(): lax.all_to_all(cells_buf, ('gx', 'gy'), split_axis=0, concat_axis=0, tile...]
  transfers between devices with their start and end apart: 12 -> 0, of which waited for: 7 -> 0; matrix products, arithmetic and copies ran while one was open for 7% -> 0% of each run, Pallas kernels for 0% -> 0%
where the time goes in v1:
time: 51.9 us; the launch traced here: 51.8 us
  Pallas kernels  51.2 us (99%)
  between operations  0.64 us (1%)
    pallas_call x1, Pallas kernels, body(): pl.pallas_call(main_kernel, out_shape=(pltpu.VMEM(field, F32), pltpu.VMEM...  47.2 us
    pallas_call x1, Pallas kernels, body(): pl.pallas_call(last_kernel, out_shape=(out, out), in_specs=[inside] * 4,...  3.99 us

profile of v1, /device:TPU:1, one launch (start us, length us, event | category | flops | bytes accessed | tf_op | source)
XLA Modules:
  0.0 51.8 jit_solution(2670195180421468376)
XLA Ops:
  0.6 47.2 %adjoint_krylov.1 = (f32[4,18,144,128]{3,2,1,0:T(8,128)S(1)}, f32[4,18,144,128]{3,2,1,0:T(8,128)S(1)}, f32[4,16,128,128]{3,2,1,0:T(8,128)S(1)}, f32[2,1,128]{2,1,0:T(1,128)S(1)}) custom-call(f32[4,16,16,1024]{3,2,1,0:T(8,128)} %na_h.1, f32[16,16,1024]{2,1,0:T(8,128)} %acc_h.1, f32[16,16,1024]{2,1,0:T(8,128)} %tx_h.1, f32[16,16,1024]{2,1,0:T(8,128)} %ty_h.1, ...), custom_call_target="tpu_custom_call" | custom-call | flops 60000000 | bytes 9000000 | tf_op jit(solution)/shard_map/adjoint_krylov/pallas_call | solution.py:400
  47.8 4.0 %adjoint_result.1 = (f32[4,16,16,1024]{3,2,1,0:T(8,128)}, f32[4,16,16,1024]{3,2,1,0:T(8,128)}) custom-call(f32[4,18,144,128]{3,2,1,0:T(8,128)S(1)} %get-tuple-element.6.b, f32[4,18,144,128]{3,2,1,0:T(8,128)S(1)} %get-tuple-element.7.q, f32[4,16,128,128]{3,2,1,0:T(8,128)S(1)} %get-tuple-element.8.w, f32[2,1,128]{2,1,0:T(1,128)S(1)} %get-tuple-element.9.sp), custom_call_target="tpu_custom_call" | custom-call | tf_op jit(solution)/shard_map/adjoint_result/pallas_call | solution.py:427

commit v2 on v1

--- a/solution.py
+++ b/solution.py
@@ -34,12 +34,12 @@
 
 
 def layer_above(ref, lead, y, here, lane):
-    nxt = ref[(*lead, pl.ds(8 * y + 1, 8), slice(None))]
+    nxt = pltpu.roll(here, 7, 0) if y == CY else ref[(*lead, pl.ds(8 * y + 1, 8), slice(None))]
     return pltpu.roll(jnp.where(lane == 0, nxt, here), 127, 1)
 
 
 def layer_below(ref, lead, y, here, lane):
-    prv = ref[(*lead, pl.ds(8 * y - 1, 8), slice(None))]
+    prv = pltpu.roll(here, 1, 0) if y == 1 else ref[(*lead, pl.ds(8 * y - 1, 8), slice(None))]
     return pltpu.roll(jnp.where(lane == 127, prv, here), 1, 1)
 
 
@@ -47,7 +47,7 @@
     na_h, acc_h, tx_h, ty_h, tz_h, own_h, site_h, lay_h, cnt_h, wi_h, mis_h,
     b, q, w, sp,
     na, co, src, diag, txc, tyc, tzc, tzm,
-    own, site, lay, cnt, wi, mis, packed, out1, in1, out2, in2, left, right, red_out, red1, red2,
+    own, site, lay, cnt, wi, mis, packed, out1, in1, out2, in2, left, right, send_x, send_y, red_out, red1, red2,
     load_sem, well_sem, s1, r1, s2, r2, hs, hr, as1, ar1, as2, ar2,
 ):
     gx, gy = lax.axis_index("gx"), lax.axis_index("gy")
@@ -171,6 +171,11 @@
     for c in second:
         c.wait()
 
+    def block(x):
+        if isinstance(x, int):
+            return K * CY * (0 if x == 0 else 1 if x == CX - 1 else x + 1)
+        return pl.multiple_of(K * CY * (x + 1), K * CY)
+
     across = in2[...].T
 
     def split(v):
@@ -178,12 +183,14 @@
         return high, (v - high)
 
     mis_high, mis_low = split(across[32:36, :])
-    spot = lax.broadcasted_iota(jnp.int32, (256, 128), 0).astype(F32) == across[36:37, :]
-    for k in RHS:
-        high = jnp.where(spot, mis_high[k : k + 1, :], 0.0).astype(BF16)
-        left[pl.ds(256 * k, 256), 0:128] = high
-        left[pl.ds(256 * k, 256), 128:256] = high
-        left[pl.ds(256 * k, 256), 256:384] = jnp.where(spot, mis_low[k : k + 1, :], 0.0).astype(BF16)
+    for x in range(CX):
+        spot = (lax.broadcasted_iota(jnp.int32, (CY, 128), 0) + CY * x).astype(F32) == across[36:37, :]
+        for k in RHS:
+            at = pl.ds(block(x) + CY * k, CY)
+            high = jnp.where(spot, mis_high[k : k + 1, :], 0.0).astype(BF16)
+            left[at, 0:128] = high
+            left[at, 128:256] = high
+            left[at, 256:384] = jnp.where(spot, mis_low[k : k + 1, :], 0.0).astype(BF16)
 
     def terms(t, _):
         lane = lanes().astype(F32)
@@ -209,12 +216,12 @@
 
     lax.fori_loop(0, 8, terms, 0)
 
-    def gather(n, _):
-        at = pl.ds(pl.multiple_of(256 * n, 256), 256)
-        src[:, at] = jnp.dot(left[...], right[:, at], preferred_element_type=F32)
-        return 0
-
-    lax.fori_loop(0, 4, gather, 0)
+    def gather(part):
+        def at(n, _):
+            here = pl.ds(pl.multiple_of(256 * n, 256), 256)
+            src[part, here] = jnp.dot(left[part, :], right[:, here], preferred_element_type=F32)
+            return 0
+        lax.fori_loop(0, NZ // 256, at, 0)
 
     for c in fields:
         c.wait()
@@ -224,23 +231,16 @@
             for t in range(2):
                 for c in range(8):
                     at = (pl.ds(8 * t, 8), pl.ds(128 * c, 128))
-                    v = co[3, x, *at] * na[k, x, *at] + src[
-                        pl.ds(pl.multiple_of(256 * k + 16 * x + 8 * t, 8), 8), pl.ds(128 * c, 128)]
+                    row = block(x) + (CY * k + 8 * t)
+                    row = row if isinstance(x, int) else pl.multiple_of(row, 8)
+                    v = co[3, x, *at] * na[k, x, *at] + src[pl.ds(row, 8), pl.ds(128 * c, 128)]
                     b[k, x + 1, pl.ds(8 + 64 * t + c, 8, stride=8), :] = v
 
-    def faces_x(f, at):
-        body = pl.ds(8, 128)
-        return [
-            remote(f.at[:, 1, body], f.at[:, CX + 1, body], hs.at[at], hr.at[at], "gx", down_x),
-            remote(f.at[:, CX, body], f.at[:, 0, body], hs.at[at + 1], hr.at[at + 1], "gx", up_x),
-        ]
-
-    def faces_y(f, at):
-        body = pl.ds(1, CX)
-        return [
-            remote(f.at[:, body, pl.ds(8, 8)], f.at[:, body, pl.ds(8 * CY + 8, 8)], hs.at[at], hr.at[at], "gy", down_y),
-            remote(f.at[:, body, pl.ds(8 * CY, 8)], f.at[:, body, pl.ds(0, 8)], hs.at[at + 1], hr.at[at + 1], "gy", up_y),
-        ]
+    def face(src_ref, dst_ref, at, axis, to):
+        return remote(src_ref, dst_ref, hs.at[at], hr.at[at], axis, to)
+
+    low, high = pl.ds(8, 8), pl.ds(8 * CY, 8)
+    before, after = pl.ds(0, 8), pl.ds(8 * CY + 8, 8)
 
     def loop(lo, hi, fn):
         def body(x, _):
@@ -248,7 +248,7 @@
             return 0
         lax.fori_loop(lo, hi, body, 0)
 
-    def apply(v, put, x, ys, sums):
+    def apply(v, put, x, ys, sums, halo=True, dots=True):
         lane = lanes()
         sums = list(sums)
         prev = None
@@ -259,66 +259,149 @@
             typ = column(tyc, cols, y)
             tzp, tzl = column(tzc, cols, y), column(tzm, cols, y - 1)
             if prev is None or prev[0] != y - 1:
-                prev = (y - 1, column(tyc, cols, y - 1), [column(v, (k, x), y - 1) for k in RHS],
+                prev = (y - 1, column(tyc, cols, y - 1), [column(v, (k, x), y - 1) if halo or y > 1 else None for k in RHS],
                         [column(v, (k, x), y) for k in RHS])
-            _, tyl, low, mid = prev
-            high = [column(v, (k, x), y + 1) for k in RHS]
+            _, tyl, down, mid = prev
+            up = [column(v, (k, x), y + 1) if halo or y < CY else None for k in RHS]
             for k in RHS:
                 here = mid[k]
-                out = (
-                    d * here
-                    - (txp * column(v, (k, x + 1), y) + txl * column(v, (k, x - 1), y))
-                    - (typ * high[k] + tyl * low[k])
-                    - (tzp * layer_above(v, (k, x), y, here, lane) + tzl * layer_below(v, (k, x), y, here, lane))
-                )
+                out = d * here
+                if halo or not (isinstance(x, int) and x == CX):
+                    out = out - txp * column(v, (k, x + 1), y)
+                if halo or not (isinstance(x, int) and x == 1):
+                    out = out - txl * column(v, (k, x - 1), y)
+                if up[k] is not None:
+                    out = out - typ * up[k]
+                if down[k] is not None:
+                    out = out - tyl * down[k]
+                out = out - (tzp * layer_above(v, (k, x), y, here, lane) + tzl * layer_below(v, (k, x), y, here, lane))
                 put(k, x, y, out)
-                sums[k] = sums[k] + here * here
-                sums[K + k] = sums[K + k] + here * out
-            prev = (y, typ, mid, high)
+                if dots:
+                    sums[k] = sums[k] + here * here
+                    sums[K + k] = sums[K + k] + here * out
+            prev = (y, typ, mid, up)
         return tuple(sums)
 
     def put_q(k, x, y, out):
         q[k, x, pl.ds(8 * y, 8), :] = out
 
+    def put_end(k, x, y, out):
+        put_q(k, x, y, out)
+        send_x[0 if x == 1 else 1, k, pl.ds(8 * (y - 1), 8), :] = out
+
+    def put_side(k, x, y, out):
+        put_q(k, x, y, out)
+        send_y[0 if y == 1 else 1, k, x - 1] = out
+
     def put_w(k, x, y, out):
         w[k, x - 1, pl.ds(8 * (y - 1), 8), :] = out
 
     def inner(v, put, sums):
         return lax.fori_loop(2, CX, lambda x, s: apply(v, put, x, range(2, CY), s), sums)
 
-    def ends(v, put, sums):
-        return lax.fori_loop(0, 2, lambda i, s: apply(v, put, 1 + (CX - 1) * i, range(1, CY + 1), s), sums)
-
-    def sides(v, put, sums):
-        return lax.fori_loop(2, CX, lambda x, s: apply(v, put, x, (1, CY), s), sums)
-
-    loop(0, 2, lambda i: begin((CX - 1) * i))
-    bx = faces_x(b, 2)
+    def ends(v, put, sums, **kw):
+        for x in (1, CX):
+            sums = apply(v, put, x, range(1, CY + 1), sums, **kw)
+        return sums
+
+    def sides(v, put, sums, **kw):
+        def at(i, s):
+            for j in range(7):
+                s = apply(v, put, 2 + 7 * i + j, (1, CY), s, **kw)
+            return s
+        return lax.fori_loop(0, 2, at, sums)
+
+    none = tuple(jnp.zeros((8, 128), F32) for _ in range(2 * K))
+    planes = pl.ds(8, 8 * CY)
+    inside_y = pl.ds(16, 8 * (CY - 2))
+    inside_x = pl.ds(2, CX - 2)
+    all_x = pl.ds(1, CX)
+
+    gather(pl.ds(0, 2 * K * CY))
+    begin(0)
+    begin(CX - 1)
+    bx = [face(b.at[:, 1, planes], b.at[:, CX + 1, planes], 2, "gx", down_x),
+          face(b.at[:, CX, planes], b.at[:, 0, planes], 3, "gx", up_x)]
     for c in bx:
         c.start()
+    gather(pl.ds(2 * K * CY, (CX - 2) * K * CY))
     loop(1, CX - 1, begin)
-    by = faces_y(b, 4)
+    by = [face(b.at[:, all_x, low], b.at[:, all_x, after], 4, "gy", down_y),
+          face(b.at[:, all_x, high], b.at[:, all_x, before], 5, "gy", up_y)]
     for c in by:
         c.start()
 
-    none = tuple(jnp.zeros((8, 128), F32) for _ in range(2 * K))
+    ends(b, put_end, none, halo=False, dots=False)
+    inner_rows = pl.ds(8, 8 * (CY - 2))
+    qx = [face(send_x.at[0, :, inner_rows], q.at[:, CX + 1, inside_y], 6, "gx", down_x),
+          face(send_x.at[1, :, inner_rows], q.at[:, 0, inside_y], 7, "gx", up_x)]
+    for c in qx:
+        c.start()
+    sides(b, put_side, none, halo=False, dots=False)
+    inner_planes = pl.ds(1, CX - 2)
+    qy = [face(send_y.at[0, :, inner_planes], q.at[:, inside_x, after], 8, "gy", down_y),
+          face(send_y.at[1, :, inner_planes], q.at[:, inside_x, before], 9, "gy", up_y)]
+    for c in qy:
+        c.start()
     one = inner(b, put_q, none)
+
+    def complete(x, y, sums):
+        sums = list(sums)
+        for k in RHS:
+            here = column(b, (k, x), y)
+            out = column(q, (k, x), y)
+            if isinstance(x, int):
+                edge = 0 if x == 1 else CX
+                out = out - column(txc, (edge,), y - 1) * column(b, (k, 0 if x == 1 else CX + 1), y)
+            if y == 1:
+                out = out - column(tyc, (x - 1,), 0) * column(b, (k, x), 0)
+            if y == CY:
+                out = out - column(tyc, (x - 1,), CY) * column(b, (k, x), CY + 1)
+            put_q(k, x, y, out)
+            sums[k] = sums[k] + here * here
+            sums[K + k] = sums[K + k] + here * out
+        return tuple(sums)
+
     for c in by + bx:
         c.wait()
-    one = ends(b, put_q, one)
-    qx = faces_x(q, 6)
-    for c in qx:
-        c.start()
-    one = sides(b, put_q, one)
-    qy = faces_y(q, 8)
+    for x in (1, CX):
+        for y in (1, CY):
+            one = complete(x, y, one)
+    corners = []
+    for i, (x, to_x, x_axis) in enumerate(((1, CX + 1, down_x), (CX, 0, up_x))):
+        for j, (y, to_y, y_axis) in enumerate(((low, after, down_y), (high, before, up_y))):
+            at = 10 + 4 * i + 2 * j
+            corners.append(face(q.at[:, x, y], q.at[:, to_x, y], at, "gx", x_axis))
+            corners.append(face(q.at[:, x, y], q.at[:, x, to_y], at + 1, "gy", y_axis))
+    for c in corners:
+        c.start()
+    for x in (1, CX):
+        for y in range(2, CY):
+            one = complete(x, y, one)
+    one = lax.fori_loop(2, CX, lambda x, s: complete(x, CY, complete(x, 1, s)), one)
+
+    two = inner(q, put_w, none)
+
+    def add(k, x, y, t, v):
+        put_q(k, x, y, column(q, (k, x), y) - t * v)
+
     for c in qy:
-        c.start()
-    two = inner(q, put_w, none)
-    for c in qy:
-        c.wait()
+        c.wait()
+
+    def beside(x, _):
+        for k in RHS:
+            add(k, x, 0, column(tyc, (x - 1,), 0), column(b, (k, x), 1))
+            add(k, x, CY + 1, column(tyc, (x - 1,), CY), column(b, (k, x), CY))
+        return 0
+
+    lax.fori_loop(2, CX, beside, 0)
     two = sides(q, put_w, two)
-    for c in qx:
-        c.wait()
+    for c in qx + corners:
+        c.wait()
+    for y in range(2, CY):
+        for k in RHS:
+            add(k, 0, y, column(txc, (0,), y - 1), column(b, (k, 1), y))
+            add(k, CX + 1, y, column(txc, (CX,), y - 1), column(b, (k, CX), y))
     two = ends(q, put_w, two)
 
     lane1 = lax.broadcasted_iota(jnp.int32, (1, 128), 1)
@@ -364,7 +447,7 @@
     ones = [jnp.broadcast_to(sp[0][:, k : k + 1], (8, 128)) for k in RHS]
     twos = [jnp.broadcast_to(sp[1][:, k : k + 1], (8, 128)) for k in RHS]
     copies = []
-    step = 4
+    step = 2
 
     def at(x, _):
         for k in RHS:
@@ -413,9 +496,10 @@
             vm((128, WELLS), F32), vm((NGY, NGX, 128), F32), vm((NGY * NGX, 128), F32),
             vm((NGX, NGY, 128), F32), vm((NGX * NGY, 128), F32),
             vm((K * CX * CY, 384), BF16), vm((384, NZ), BF16),
+            vm((2, K, 8 * CY, 128), F32), vm((2, K, CX, 8, 128), F32),
             vm((2, 1, 128), F32), vm((NGX, 1, 128), F32), vm((NGY, 1, 128), F32),
             dma((8,)), dma((6,)), dma((NGY,)), dma((NGY,)), dma((NGX,)), dma((NGX,)),
-            dma((10,)), dma((10,)), dma((NGX,)), dma((NGX,)), dma((NGY,)), dma((NGY,)),
+            dma((18,)), dma((18,)), dma((NGX,)), dma((NGX,)), dma((NGY,)), dma((NGY,)),
         ],
         compiler_params=pltpu.CompilerParams(
             collective_id=0, has_side_effects=True, vmem_limit_bytes=40 * 2**20),
@@ -429,7 +513,7 @@
         out_shape=(out, out),
         in_specs=[inside] * 4,
         out_specs=(anywhere, anywhere),
-        scratch_shapes=[vm((K, CX, CY, NZ), F32), vm((K, CX, CY, NZ), F32), dma((8,))],
+        scratch_shapes=[vm((K, CX, CY, NZ), F32), vm((K, CX, CY, NZ), F32), dma((16,))],
         compiler_params=pltpu.CompilerParams(vmem_limit_bytes=24 * 2**20),
         name="adjoint_result",
     )(b, q, w, sp)

time: 51.9 us -> 48.2 us (0.929)
  Pallas kernels: 51.2 us -> 47.4 us
    pallas_call x1, Pallas kernels: 47.2 us -> 43.7 us  [body(): pl.pallas_call(main_kernel, out_shape=(pltpu.VMEM(field, F32), pltpu.VMEM...]
where the time goes in v2:
time: 48.2 us; the launch traced here: 48.1 us
  Pallas kernels  47.4 us (98%)
  between operations  0.64 us (1%)
    pallas_call x1, Pallas kernels, body(): pl.pallas_call(main_kernel, out_shape=(pltpu.VMEM(field, F32), pltpu.VMEM...  43.7 us
    pallas_call x1, Pallas kernels, body(): pl.pallas_call(last_kernel, out_shape=(out, out), in_specs=[inside] * 4,...  3.76 us

profile of v2, /device:TPU:1, one launch (start us, length us, event | category | flops | bytes accessed | tf_op | source)
XLA Modules:
  0.0 48.1 jit_solution(6990860853320993278)
XLA Ops:
  0.6 43.7 %adjoint_krylov.1 = (f32[4,18,144,128]{3,2,1,0:T(8,128)S(1)}, f32[4,18,144,128]{3,2,1,0:T(8,128)S(1)}, f32[4,16,128,128]{3,2,1,0:T(8,128)S(1)}, f32[2,1,128]{2,1,0:T(1,128)S(1)}) custom-call(f32[4,16,16,1024]{3,2,1,0:T(8,128)} %na_h.1, f32[16,16,1024]{2,1,0:T(8,128)} %acc_h.1, f32[16,16,1024]{2,1,0:T(8,128)} %tx_h.1, f32[16,16,1024]{2,1,0:T(8,128)} %ty_h.1, ...), custom_call_target="tpu_custom_call" | custom-call | flops 60000000 | bytes 9000000 | tf_op jit(solution)/shard_map/adjoint_krylov/pallas_call | solution.py:483
  44.3 3.8 %adjoint_result.1 = (f32[4,16,16,1024]{3,2,1,0:T(8,128)}, f32[4,16,16,1024]{3,2,1,0:T(8,128)}) custom-call(f32[4,18,144,128]{3,2,1,0:T(8,128)S(1)} %get-tuple-element.6.b, f32[4,18,144,128]{3,2,1,0:T(8,128)S(1)} %get-tuple-element.7.q, f32[4,16,128,128]{3,2,1,0:T(8,128)S(1)} %get-tuple-element.8.w, f32[2,1,128]{2,1,0:T(1,128)S(1)} %get-tuple-element.9.sp), custom_call_target="tpu_custom_call" | custom-call | tf_op jit(solution)/shard_map/adjoint_result/pallas_call | solution.py:511

commit v3 on v2

--- a/solution.py
+++ b/solution.py
@@ -58,13 +58,6 @@
         ((own_h, own), (site_h, site), (lay_h, lay), (cnt_h, cnt), (wi_h, wi), (mis_h, mis)))]
     for c in wells:
         c.start()
-    coef = [pltpu.make_async_copy(h, co.at[i], load_sem.at[i]) for i, h in enumerate((tx_h, ty_h, tz_h, acc_h))]
-    for c in coef:
-        c.start()
-    fields = [pltpu.make_async_copy(na_h.at[k], na.at[k], load_sem.at[4 + k]) for k in RHS]
-    for c in fields:
-        c.start()
-
     barrier = pltpu.get_barrier_semaphore()
     for d in range(1, NGY):
         pl.semaphore_signal(barrier, inc=1, device_id={"gy": lax.rem(gy + d, NGY)}, device_id_type=MESH)
@@ -95,6 +88,13 @@
         first.append(remote(out1.at[to], in1.at[pl.ds(gy * NGX, NGX)], s1.at[d], r1.at[d], "gy", to))
     for c in first:
         c.start()
+    coef = [pltpu.make_async_copy(h, co.at[i], load_sem.at[i]) for i, h in enumerate((tx_h, ty_h, tz_h, acc_h))]
+    for c in coef:
+        c.start()
+    fields = [pltpu.make_async_copy(na_h.at[k], na.at[k], load_sem.at[4 + k]) for k in RHS]
+    for c in fields:
+        c.start()
+
     in1[pl.ds(gy * NGX, NGX), :] = out1[gy]
 
     last_x = gx == NGX - 1
@@ -287,6 +287,8 @@
 
     def put_end(k, x, y, out):
         put_q(k, x, y, out)
+        if y in (1, CY):
+            return
         send_x[0 if x == 1 else 1, k, pl.ds(8 * (y - 1), 8), :] = out
 
     def put_side(k, x, y, out):
@@ -295,9 +297,6 @@
 
     def put_w(k, x, y, out):
         w[k, x - 1, pl.ds(8 * (y - 1), 8), :] = out
-
-    def inner(v, put, sums):
-        return lax.fori_loop(2, CX, lambda x, s: apply(v, put, x, range(2, CY), s), sums)
 
     def ends(v, put, sums, **kw):
         for x in (1, CX):
@@ -317,33 +316,62 @@
     inside_x = pl.ds(2, CX - 2)
     all_x = pl.ds(1, CX)
 
+    both = ((1, CX + 1, 0, 0, down_x), (CX, 0, 1, CX, up_x))
+    both_y = ((low, after, 0, 1, down_y), (high, before, 1, CY, up_y))
+
     gather(pl.ds(0, 2 * K * CY))
     begin(0)
     begin(CX - 1)
-    bx = [face(b.at[:, 1, planes], b.at[:, CX + 1, planes], 2, "gx", down_x),
-          face(b.at[:, CX, planes], b.at[:, 0, planes], 3, "gx", up_x)]
+    tips = []
+    for i, (x, to_x, _, _, x_axis) in enumerate(both):
+        for j, (y, to_y, _, _, y_axis) in enumerate(both_y):
+            at = 10 + 4 * i + 2 * j
+            tips.append(face(b.at[:, x, y], b.at[:, to_x, y], at, "gx", x_axis))
+            tips.append(face(b.at[:, x, y], b.at[:, x, to_y], at + 1, "gy", y_axis))
+    for c in tips:
+        c.start()
+    bx = [face(b.at[:, x, inside_y], b.at[:, to_x, inside_y], 2 + i, "gx", axis)
+          for i, (x, to_x, _, _, axis) in enumerate(both)]
     for c in bx:
         c.start()
-    gather(pl.ds(2 * K * CY, (CX - 2) * K * CY))
-    loop(1, CX - 1, begin)
-    by = [face(b.at[:, all_x, low], b.at[:, all_x, after], 4, "gy", down_y),
-          face(b.at[:, all_x, high], b.at[:, all_x, before], 5, "gy", up_y)]
-    for c in by:
-        c.start()
+    by = []
+    for part, some in enumerate((range(1, CX // 2), range(CX // 2, CX - 1))):
+        gather(pl.ds(block(some[0]), len(some) * K * CY))
+        loop(some[0], some[-1] + 1, begin)
+        here = pl.ds(some[0] + 1, len(some))
+        for i, (y, to_y, _, _, axis) in enumerate(both_y):
+            c = face(b.at[:, here, y], b.at[:, here, to_y], (4 if part == 0 else 22) + i, "gy", axis)
+            c.start()
+            by.append(c)
 
     ends(b, put_end, none, halo=False, dots=False)
-    inner_rows = pl.ds(8, 8 * (CY - 2))
-    qx = [face(send_x.at[0, :, inner_rows], q.at[:, CX + 1, inside_y], 6, "gx", down_x),
-          face(send_x.at[1, :, inner_rows], q.at[:, 0, inside_y], 7, "gx", up_x)]
-    for c in qx:
-        c.start()
     sides(b, put_side, none, halo=False, dots=False)
-    inner_planes = pl.ds(1, CX - 2)
-    qy = [face(send_y.at[0, :, inner_planes], q.at[:, inside_x, after], 8, "gy", down_y),
-          face(send_y.at[1, :, inner_planes], q.at[:, inside_x, before], 9, "gy", up_y)]
+    for c in tips:
+        c.wait()
+    for x, _, i, x_edge, _ in both:
+        for _, _, j, y, _ in both_y:
+            for k in RHS:
+                here = column(q, (k, x), y)
+                far_y = column(tyc, (x - 1,), 0 if y == 1 else CY) * column(b, (k, x), 0 if y == 1 else CY + 1)
+                far_x = column(txc, (x_edge,), y - 1) * column(b, (k, 0 if x == 1 else CX + 1), y)
+                send_x[i, k, pl.ds(8 * (y - 1), 8), :] = here - far_y
+                send_y[j, k, x - 1] = here - far_x
+    qy = [face(send_y.at[j], q.at[:, all_x, to_y], 8 + j, "gy", axis)
+          for j, (_, to_y, _, _, axis) in enumerate(both_y)]
     for c in qy:
         c.start()
-    one = inner(b, put_q, none)
+    first_half, second_half = [], []
+    for i, (_, to_x, _, _, axis) in enumerate(both):
+        for half in range(2):
+            ks = pl.ds(2 * half, 2)
+            c = face(send_x.at[i, ks], q.at[ks, to_x, planes], 18 + 2 * i + half, "gx", axis)
+            (second_half if i == half else first_half).append(c)
+    one = lax.fori_loop(2, 6, lambda x, s: apply(b, put_q, x, range(2, CY), s), none)
+    for c in first_half:
+        c.start()
+    one = lax.fori_loop(6, CX, lambda x, s: apply(b, put_q, x, range(2, CY), s), one)
+
+    two = lax.fori_loop(3, CX - 1, lambda x, s: apply(q, put_w, x, range(3, CY - 1), s), none)
 
     def complete(x, y, sums):
         sums = list(sums)
@@ -365,44 +393,55 @@
     for c in by + bx:
         c.wait()
     for x in (1, CX):
-        for y in (1, CY):
-            one = complete(x, y, one)
-    corners = []
-    for i, (x, to_x, x_axis) in enumerate(((1, CX + 1, down_x), (CX, 0, up_x))):
-        for j, (y, to_y, y_axis) in enumerate(((low, after, down_y), (high, before, up_y))):
-            at = 10 + 4 * i + 2 * j
-            corners.append(face(q.at[:, x, y], q.at[:, to_x, y], at, "gx", x_axis))
-            corners.append(face(q.at[:, x, y], q.at[:, x, to_y], at + 1, "gy", y_axis))
-    for c in corners:
-        c.start()
-    for x in (1, CX):
-        for y in range(2, CY):
+        for y in range(1, CY + 1):
             one = complete(x, y, one)
     one = lax.fori_loop(2, CX, lambda x, s: complete(x, CY, complete(x, 1, s)), one)
-
-    two = inner(q, put_w, none)
-
-    def add(k, x, y, t, v):
-        put_q(k, x, y, column(q, (k, x), y) - t * v)
+    for c in second_half:
+        c.start()
+
+    def ring(i, s):
+        for j in range(4):
+            s = apply(q, put_w, 3 + 4 * i + j, (1, 2, CY - 1, CY), s, halo=False)
+        return s
+
+    two = lax.fori_loop(0, (CX - 4) // 4, ring, two)
+    for x in (1, 2, CX - 1, CX):
+        two = apply(q, put_w, x, range(1, CY + 1), two, halo=False)
+
+    def meet(k, x, y, t, far, sums):
+        other = t * (far - t * column(b, (k, x), y))
+        at = (k, x - 1, pl.ds(8 * (y - 1), 8), slice(None))
+        w[at] = w[at] - other
+        if sums is not None:
+            sums[K + k] = sums[K + k] - 2.0 * (column(q, (k, x), y) * other)
+
+    def meet_x(i, ks, sums):
+        x, x_far, edge = ((1, 0, 0), (CX, CX + 1, CX))[i]
+        for y in range(1, CY + 1):
+            t = column(txc, (edge,), y - 1)
+            for k in ks:
+                meet(k, x, y, t, column(q, (k, x_far), y), sums)
+
+    def meet_y(y, x, sums):
+        t = column(tyc, (x - 1,), 0 if y == 1 else CY)
+        for k in RHS:
+            meet(k, x, y, t, column(q, (k, x), 0 if y == 1 else CY + 1), sums)
 
     for c in qy:
         c.wait()
 
-    def beside(x, _):
-        for k in RHS:
-            add(k, x, 0, column(tyc, (x - 1,), 0), column(b, (k, x), 1))
-            add(k, x, CY + 1, column(tyc, (x - 1,), CY), column(b, (k, x), CY))
-        return 0
-
-    lax.fori_loop(2, CX, beside, 0)
-    two = sides(q, put_w, two)
-    for c in qx + corners:
-        c.wait()
-    for y in range(2, CY):
-        for k in RHS:
-            add(k, 0, y, column(txc, (0,), y - 1), column(b, (k, 1), y))
-            add(k, CX + 1, y, column(txc, (CX,), y - 1), column(b, (k, CX), y))
-    two = ends(q, put_w, two)
+    def lower_y(i, sums):
+        sums = list(sums)
+        for j in range(4):
+            meet_y(1, 1 + 4 * i + j, sums)
+        return tuple(sums)
+
+    two = list(lax.fori_loop(0, CX // 4, lower_y, two))
+    for c in first_half:
+        c.wait()
+    meet_x(0, (0, 1), two)
+    meet_x(1, (2, 3), two)
+    two = tuple(two)
 
     lane1 = lax.broadcasted_iota(jnp.int32, (1, 128), 1)
     line = jnp.zeros((1, 128), F32)
@@ -416,6 +455,11 @@
         hops.append(remote(red_out.at[0], red1.at[gx], as1.at[d], ar1.at[d], "gx", to))
     for c in hops:
         c.start()
+    loop(1, CX + 1, lambda x: meet_y(CY, x, None))
+    for c in second_half:
+        c.wait()
+    meet_x(0, (2, 3), None)
+    meet_x(1, (0, 1), None)
     for c in hops:
         c.wait()
     line = jnp.sum(red1[...], axis=0)
@@ -499,7 +543,7 @@
             vm((2, K, 8 * CY, 128), F32), vm((2, K, CX, 8, 128), F32),
             vm((2, 1, 128), F32), vm((NGX, 1, 128), F32), vm((NGY, 1, 128), F32),
             dma((8,)), dma((6,)), dma((NGY,)), dma((NGY,)), dma((NGX,)), dma((NGX,)),
-            dma((18,)), dma((18,)), dma((NGX,)), dma((NGX,)), dma((NGY,)), dma((NGY,)),
+            dma((24,)), dma((24,)), dma((NGX,)), dma((NGX,)), dma((NGY,)), dma((NGY,)),
         ],
         compiler_params=pltpu.CompilerParams(
             collective_id=0, has_side_effects=True, vmem_limit_bytes=40 * 2**20),

time: 48.2 us -> 45.4 us (0.942)
  Pallas kernels: 47.4 us -> 44.6 us
    pallas_call x1, Pallas kernels: 43.7 us -> 40.8 us  [body(): pl.pallas_call(main_kernel, out_shape=(pltpu.VMEM(field, F32), pltpu.VMEM...]
where the time goes in v3:
time: 45.4 us; the launch traced here: 45.2 us
  Pallas kernels  44.6 us (98%)
  between operations  0.64 us (1%)
    pallas_call x1, Pallas kernels, body(): pl.pallas_call(main_kernel, out_shape=(pltpu.VMEM(field, F32), pltpu.VMEM...  40.8 us
    pallas_call x1, Pallas kernels, body(): pl.pallas_call(last_kernel, out_shape=(out, out), in_specs=[inside] * 4,...  3.76 us

profile of v3, /device:TPU:1, one launch (start us, length us, event | category | flops | bytes accessed | tf_op | source)
XLA Modules:
  0.0 45.2 jit_solution(11504591712980406502)
XLA Ops:
  0.6 40.8 %adjoint_krylov.1 = (f32[4,18,144,128]{3,2,1,0:T(8,128)S(1)}, f32[4,18,144,128]{3,2,1,0:T(8,128)S(1)}, f32[4,16,128,128]{3,2,1,0:T(8,128)S(1)}, f32[2,1,128]{2,1,0:T(1,128)S(1)}) custom-call(f32[4,16,16,1024]{3,2,1,0:T(8,128)} %na_h.1, f32[16,16,1024]{2,1,0:T(8,128)} %acc_h.1, f32[16,16,1024]{2,1,0:T(8,128)} %tx_h.1, f32[16,16,1024]{2,1,0:T(8,128)} %ty_h.1, ...), custom_call_target="tpu_custom_call" | custom-call | flops 60000000 | bytes 9000000 | tf_op jit(solution)/shard_map/adjoint_krylov/pallas_call | solution.py:527
  41.5 3.8 %adjoint_result.1 = (f32[4,16,16,1024]{3,2,1,0:T(8,128)}, f32[4,16,16,1024]{3,2,1,0:T(8,128)}) custom-call(f32[4,18,144,128]{3,2,1,0:T(8,128)S(1)} %get-tuple-element.6.b, f32[4,18,144,128]{3,2,1,0:T(8,128)S(1)} %get-tuple-element.7.q, f32[4,16,128,128]{3,2,1,0:T(8,128)S(1)} %get-tuple-element.8.w, f32[2,1,128]{2,1,0:T(1,128)S(1)} %get-tuple-element.9.sp), custom_call_target="tpu_custom_call" | custom-call | tf_op jit(solution)/shard_map/adjoint_result/pallas_call | solution.py:555

commit v4 on v3

--- a/solution.py
+++ b/solution.py
@@ -168,29 +168,9 @@
 
     lax.fori_loop(0, CX, diagonal, 0)
 
-    for c in second:
-        c.wait()
-
-    def block(x):
-        if isinstance(x, int):
-            return K * CY * (0 if x == 0 else 1 if x == CX - 1 else x + 1)
-        return pl.multiple_of(K * CY * (x + 1), K * CY)
-
-    across = in2[...].T
-
     def split(v):
         high = v.astype(BF16).astype(F32)
         return high, (v - high)
-
-    mis_high, mis_low = split(across[32:36, :])
-    for x in range(CX):
-        spot = (lax.broadcasted_iota(jnp.int32, (CY, 128), 0) + CY * x).astype(F32) == across[36:37, :]
-        for k in RHS:
-            at = pl.ds(block(x) + CY * k, CY)
-            high = jnp.where(spot, mis_high[k : k + 1, :], 0.0).astype(BF16)
-            left[at, 0:128] = high
-            left[at, 128:256] = high
-            left[at, 256:384] = jnp.where(spot, mis_low[k : k + 1, :], 0.0).astype(BF16)
 
     def terms(t, _):
         lane = lanes().astype(F32)
@@ -214,7 +194,41 @@
         right[pl.ds(pl.multiple_of(256 + 16 * t, 16), 16), :] = high
         return 0
 
-    lax.fori_loop(0, 8, terms, 0)
+    def arrived(source):
+        d = lax.rem(gx + NGX - source, NGX)
+        remote(out2.at[0], in2.at[pl.ds(source * NGY, NGY)], s2.at[d], r2.at[d], "gx", source).wait_recv()
+
+    arrived(gx + 1 - 2 * lax.rem(gx, 2))
+    terms(gx // 2, 0)
+
+    def next_tile(j, _):
+        i = j // 2
+        t = 2 * lax.rem(gx // 4 + i * (i + 1) // 2, 4) + lax.rem(lax.rem(gx, 4) // 2 + j, 2)
+        arrived(2 * t)
+        arrived(2 * t + 1)
+        return terms(t, 0)
+
+    lax.fori_loop(1, NGX // 2, next_tile, 0)
+    for c in second:
+        c.wait_send()
+
+
+    def block(x):
+        if isinstance(x, int):
+            return K * CY * (0 if x == 0 else 1 if x == CX - 1 else x + 1)
+        return pl.multiple_of(K * CY * (x + 1), K * CY)
+
+    across = in2[...].T
+
+    mis_high, mis_low = split(across[32:36, :])
+    for x in range(CX):
+        spot = (lax.broadcasted_iota(jnp.int32, (CY, 128), 0) + CY * x).astype(F32) == across[36:37, :]
+        for k in RHS:
+            at = pl.ds(block(x) + CY * k, CY)
+            high = jnp.where(spot, mis_high[k : k + 1, :], 0.0).astype(BF16)
+            left[at, 0:128] = high
+            left[at, 128:256] = high
+            left[at, 256:384] = jnp.where(spot, mis_low[k : k + 1, :], 0.0).astype(BF16)
 
     def gather(part):
         def at(n, _):

time: 45.4 us -> 44.7 us (0.985)
  Pallas kernels: 44.6 us -> 43.9 us
    pallas_call x1, Pallas kernels: 40.8 us -> 40.2 us  [body(): pl.pallas_call(main_kernel, out_shape=(pltpu.VMEM(field, F32), pltpu.VMEM...]
where the time goes in v4:
time: 44.7 us; the launch traced here: 44.6 us
  Pallas kernels  43.9 us (98%)
  between operations  0.64 us (1%)
    pallas_call x1, Pallas kernels, body(): pl.pallas_call(main_kernel, out_shape=(pltpu.VMEM(field, F32), pltpu.VMEM...  40.2 us
    pallas_call x1, Pallas kernels, body(): pl.pallas_call(last_kernel, out_shape=(out, out), in_specs=[inside] * 4,...  3.76 us

profile of v4, /device:TPU:1, one launch (start us, length us, event | category | flops | bytes accessed | tf_op | source)
XLA Modules:
  0.0 44.6 jit_solution(13496657181640404292)
XLA Ops:
  0.6 40.2 %adjoint_krylov.1 = (f32[4,18,144,128]{3,2,1,0:T(8,128)S(1)}, f32[4,18,144,128]{3,2,1,0:T(8,128)S(1)}, f32[4,16,128,128]{3,2,1,0:T(8,128)S(1)}, f32[2,1,128]{2,1,0:T(1,128)S(1)}) custom-call(f32[4,16,16,1024]{3,2,1,0:T(8,128)} %na_h.1, f32[16,16,1024]{2,1,0:T(8,128)} %acc_h.1, f32[16,16,1024]{2,1,0:T(8,128)} %tx_h.1, f32[16,16,1024]{2,1,0:T(8,128)} %ty_h.1, ...), custom_call_target="tpu_custom_call" | custom-call | flops 60000000 | bytes 9000000 | tf_op jit(solution)/shard_map/adjoint_krylov/pallas_call | solution.py:541
  40.8 3.8 %adjoint_result.1 = (f32[4,16,16,1024]{3,2,1,0:T(8,128)}, f32[4,16,16,1024]{3,2,1,0:T(8,128)}) custom-call(f32[4,18,144,128]{3,2,1,0:T(8,128)S(1)} %get-tuple-element.6.b, f32[4,18,144,128]{3,2,1,0:T(8,128)S(1)} %get-tuple-element.7.q, f32[4,16,128,128]{3,2,1,0:T(8,128)S(1)} %get-tuple-element.8.w, f32[2,1,128]{2,1,0:T(1,128)S(1)} %get-tuple-element.9.sp), custom_call_target="tpu_custom_call" | custom-call | tf_op jit(solution)/shard_map/adjoint_result/pallas_call | solution.py:569

commit v5 on v4

--- a/solution.py
+++ b/solution.py
@@ -92,8 +92,6 @@
     for c in coef:
         c.start()
     fields = [pltpu.make_async_copy(na_h.at[k], na.at[k], load_sem.at[4 + k]) for k in RHS]
-    for c in fields:
-        c.start()
 
     in1[pl.ds(gy * NGX, NGX), :] = out1[gy]
 
@@ -141,6 +139,8 @@
         to = lax.rem(gx + d, NGX)
         second.append(remote(out2.at[to], in2.at[pl.ds(gx * NGY, NGY)], s2.at[d], r2.at[d], "gx", to))
     for c in second:
+        c.start()
+    for c in fields:
         c.start()
     in2[pl.ds(gx * NGY, NGY), :] = out2[gx]
 

time: 44.7 us -> 44.7 us (level)
  no operation moved by 1% of the time
where the time goes in v5:
time: 44.7 us; the launch traced here: 44.6 us
  Pallas kernels  43.9 us (98%)
  between operations  0.64 us (1%)
    pallas_call x1, Pallas kernels, body(): pl.pallas_call(main_kernel, out_shape=(pltpu.VMEM(field, F32), pltpu.VMEM...  40.2 us
    pallas_call x1, Pallas kernels, body(): pl.pallas_call(last_kernel, out_shape=(out, out), in_specs=[inside] * 4,...  3.76 us

profile of v5, /device:TPU:1, one launch (start us, length us, event | category | flops | bytes accessed | tf_op | source)
XLA Modules:
  0.0 44.6 jit_solution(11653653621065258265)
XLA Ops:
  0.6 40.2 %adjoint_krylov.1 = (f32[4,18,144,128]{3,2,1,0:T(8,128)S(1)}, f32[4,18,144,128]{3,2,1,0:T(8,128)S(1)}, f32[4,16,128,128]{3,2,1,0:T(8,128)S(1)}, f32[2,1,128]{2,1,0:T(1,128)S(1)}) custom-call(f32[4,16,16,1024]{3,2,1,0:T(8,128)} %na_h.1, f32[16,16,1024]{2,1,0:T(8,128)} %acc_h.1, f32[16,16,1024]{2,1,0:T(8,128)} %tx_h.1, f32[16,16,1024]{2,1,0:T(8,128)} %ty_h.1, ...), custom_call_target="tpu_custom_call" | custom-call | flops 60000000 | bytes 9000000 | tf_op jit(solution)/shard_map/adjoint_krylov/pallas_call | solution.py:541
  40.8 3.8 %adjoint_result.1 = (f32[4,16,16,1024]{3,2,1,0:T(8,128)}, f32[4,16,16,1024]{3,2,1,0:T(8,128)}) custom-call(f32[4,18,144,128]{3,2,1,0:T(8,128)S(1)} %get-tuple-element.6.b, f32[4,18,144,128]{3,2,1,0:T(8,128)S(1)} %get-tuple-element.7.q, f32[4,16,128,128]{3,2,1,0:T(8,128)S(1)} %get-tuple-element.8.w, f32[2,1,128]{2,1,0:T(1,128)S(1)} %get-tuple-element.9.sp), custom_call_target="tpu_custom_call" | custom-call | tf_op jit(solution)/shard_map/adjoint_result/pallas_call | solution.py:569
